TPU v7x, 128 devices: a whole 4x4x4 slice. The times are simulated.
128 devices in a mesh: ctx: 32 (over x, y_hi, z), tp: 4 (over y_lo, core).
Axes of the slice: x: 4, y: 4 (y_hi: 2, y_lo: 2; y = y_hi * 2 + y_lo), z: 4, core: 2. Of those that a mesh axis runs over, the one named last changes fastest.
Arguments:
- tokens: bfloat16 [8192, 2048], P('ctx'), may hold values from -6 to 6
- query_weight: bfloat16 [2048, 2048], P(None, 'tp'), may hold values from -0.125 to 0.125
- key_weight: bfloat16 [2048, 2048], P(None, 'tp'), may hold values from -0.125 to 0.125
- value_weight: bfloat16 [2048, 2048], P(None, 'tp'), may hold values from -0.125 to 0.125
- output_weight: bfloat16 [2048, 2048], P('tp'), may hold values from -0.125 to 0.125
- gate_weight: bfloat16 [2048, 8192], P(None, 'tp'), may hold values from -0.125 to 0.125
- up_weight: bfloat16 [2048, 8192], P(None, 'tp'), may hold values from -0.125 to 0.125
- down_weight: bfloat16 [8192, 2048], P('tp'), may hold values from -0.0625 to 0.0625
- query_gain: float32 [2048], P('tp'), may hold values from 0.5 to 1.5
- key_gain: float32 [2048], P('tp'), may hold values from 0.5 to 1.5
- attention_gain: float32 [2048], replicated, may hold values from 0.5 to 1.5
- feedforward_gain: float32 [2048], replicated, may hold values from 0.5 to 1.5
- cotangent: bfloat16 [8192, 2048], P('ctx'), may hold values from -6 to 6
Outputs:
- layer_output: bfloat16 [8192, 2048], P('ctx')
- tokens_grad: float32 [8192, 2048], P('ctx')
- query_weight_grad: float32 [2048, 2048], P('ctx', 'tp')
- key_weight_grad: float32 [2048, 2048], P('ctx', 'tp')
- value_weight_grad: float32 [2048, 2048], P('ctx', 'tp')
- output_weight_grad: float32 [2048, 2048], P('tp', 'ctx')
- gate_weight_grad: float32 [2048, 8192], P('ctx', 'tp')
- up_weight_grad: float32 [2048, 8192], P('ctx', 'tp')
- down_weight_grad: float32 [8192, 2048], P('tp', 'ctx')
- query_gain_grad: float32 [2048], P('tp')
- key_gain_grad: float32 [2048], P('tp')
- attention_gain_grad: float32 [2048], replicated
- feedforward_gain_grad: float32 [2048], replicated
All inputs are finite; a program needn't handle non-finite values.
Results may differ from a plain program's by a relative error of at most 0.035.
Values may be sent and summed in bfloat16 or wider, within the bound.
No kernel may reach another device: no remote copies, remote signals or barrier semaphores. Data moves between devices by JAX's collectives and lax.ppermute only.
A program may use at most 256 MiB of HBM per device.

v0:
```python
import math

import jax
import jax.numpy as jnp
from jax import lax
from jax.sharding import PartitionSpec as P

HD = 128


epsilon = 1e-06
rope_base = 500000.0
negative = -1e30


def product(left, right):
    return jnp.dot(left, right, preferred_element_type=jnp.float32)


def product_left(left, right):
    return lax.dot_general(
        left, right, (((0,), (0,)), ((), ())), preferred_element_type=jnp.float32
    )


def product_right(left, right):
    return lax.dot_general(
        left, right, (((1,), (1,)), ((), ())), preferred_element_type=jnp.float32
    )


def rope_tables(positions, head_size):
    half_size = head_size // 2
    frequency = 1.0 / rope_base ** (jnp.arange(half_size, dtype=jnp.float32) * 2.0 / head_size)
    angles = positions.astype(jnp.float32)[:, None] * frequency[None, :]
    return (jnp.cos(angles)[:, None, :], jnp.sin(angles)[:, None, :])


def rotate(values_in, cosine_table, sine_table):
    half_size = values_in.shape[-1] // 2
    lower_half = values_in[..., :half_size]
    upper_half = values_in[..., half_size:]
    return jnp.concatenate(
        [
            lower_half * cosine_table - upper_half * sine_table,
            upper_half * cosine_table + lower_half * sine_table,
        ],
        axis=-1,
    )


def rotate_back(values_in, cosine_table, sine_table):
    half_size = values_in.shape[-1] // 2
    lower_half = values_in[..., :half_size]
    upper_half = values_in[..., half_size:]
    return jnp.concatenate(
        [
            lower_half * cosine_table + upper_half * sine_table,
            upper_half * cosine_table - lower_half * sine_table,
        ],
        axis=-1,
    )


def norm_back(values_in, scale_in, gain_in, grad_in):
    scaled_grad = grad_in * gain_in
    inner = jnp.mean(scaled_grad * values_in, axis=-1, keepdims=True)
    return scale_in * scaled_grad - values_in * scale_in**3 * inner


def per_device(
    tokens,
    query_weight,
    key_weight,
    value_weight,
    output_weight,
    gate_weight,
    up_weight,
    down_weight,
    query_gain,
    key_gain,
    attention_gain,
    feedforward_gain,
    cotangent,
):
    row_count = tokens.shape[0]
    full_width = tokens.shape[1]
    local_width = query_weight.shape[1]
    head_count = local_width // HD
    score_scale = 1.0 / math.sqrt(HD)
    length = row_count * lax.axis_size("ctx")
    first_row = lax.axis_index("ctx") * row_count
    last_row = first_row + row_count - 1
    positions = first_row + jnp.arange(row_count, dtype=jnp.int32)
    cosine_table, sine_table = rope_tables(positions, HD)
    inputs = tokens.astype(jnp.float32)
    query_raw = product(tokens, query_weight)
    key_raw = product(tokens, key_weight)
    value_low = product(tokens, value_weight).astype(jnp.bfloat16)
    query_square, key_square = lax.psum(
        (jnp.sum(query_raw * query_raw, axis=1), jnp.sum(key_raw * key_raw, axis=1)), "tp"
    )
    query_scale = lax.rsqrt(query_square / full_width + epsilon)[:, None]
    key_scale = lax.rsqrt(key_square / full_width + epsilon)[:, None]
    query_low = rotate(
        (query_raw * query_scale * query_gain).reshape(row_count, head_count, HD),
        cosine_table,
        sine_table,
    ).astype(jnp.bfloat16)
    key_low = (
        rotate(
            (key_raw * key_scale * key_gain).reshape(row_count, head_count, HD),
            cosine_table,
            sine_table,
        )
        .astype(jnp.bfloat16)
        .reshape(row_count, local_width)
    )
    start_state = (
        jnp.full((head_count, row_count), negative, jnp.float32),
        jnp.zeros((head_count, row_count), jnp.float32),
        jnp.zeros((row_count, head_count, HD), jnp.float32),
    )
    remote_keys = lax.all_gather(key_low, "ctx", axis=0, tiled=True)
    remote_values = lax.all_gather(value_low, "ctx", axis=0, tiled=True)
    key_count = remote_keys.shape[0]

    def attend_compute(state_now):
        row_max, row_total, summed = state_now
        keys_heads = remote_keys.reshape(key_count, head_count, HD)
        values_heads = remote_values.reshape(key_count, head_count, HD)
        scores = (
            jnp.einsum("qhd,khd->hqk", query_low, keys_heads, preferred_element_type=jnp.float32)
            * score_scale
        )
        key_pos = jnp.arange(key_count, dtype=jnp.int32)
        visible = key_pos[None, :] <= positions[:, None]
        masked = jnp.where(visible[None], scores, negative)
        new_max = jnp.maximum(row_max, jnp.max(masked, axis=-1))
        weights = jnp.where(visible[None], jnp.exp(masked - new_max[..., None]), 0.0)
        row_total = jnp.sum(weights, axis=-1)
        summed = jnp.einsum(
            "hqk,khd->qhd",
            weights.astype(jnp.bfloat16),
            values_heads,
            preferred_element_type=jnp.float32,
        )
        return (new_max, row_total, summed)

    def passing(state_now):
        return state_now

    row_max, row_total, summed = lax.cond(
        jnp.int32(0) <= last_row, attend_compute, passing, start_state
    )
    context = summed / jnp.transpose(row_total)[:, :, None]
    context_low = context.reshape(row_count, local_width).astype(jnp.bfloat16)
    log_total = row_max + jnp.log(row_total)
    attn_sum = lax.psum(product(context_low, output_weight).astype(jnp.bfloat16), "tp").astype(
        jnp.float32
    )
    attn_scale = lax.rsqrt(jnp.mean(attn_sum * attn_sum, axis=-1, keepdims=True) + epsilon)
    hidden = inputs + attn_sum * attn_scale * attention_gain
    hidden_low = hidden.astype(jnp.bfloat16)
    gate_act = product(hidden_low, gate_weight)
    up_act = product(hidden_low, up_weight)
    gate_sigmoid = jax.nn.sigmoid(gate_act)
    gate_silu = gate_act * gate_sigmoid
    mixed_low = (gate_silu * up_act).astype(jnp.bfloat16)
    ffn_sum = lax.psum(product(mixed_low, down_weight).astype(jnp.bfloat16), "tp").astype(
        jnp.float32
    )
    ffn_scale = lax.rsqrt(jnp.mean(ffn_sum * ffn_sum, axis=-1, keepdims=True) + epsilon)
    layer_output = hidden + ffn_sum * ffn_scale * feedforward_gain
    upstream = cotangent.astype(jnp.float32)
    ffn_gain_term = jnp.sum(upstream * ffn_sum * ffn_scale, axis=0)
    ffn_grad = norm_back(ffn_sum, ffn_scale, feedforward_gain, upstream).astype(jnp.bfloat16)
    down_term = product_left(mixed_low, ffn_grad)
    mixed_grad = product_right(ffn_grad, down_weight)
    gate_grad = (
        mixed_grad * up_act * gate_sigmoid * (1.0 + gate_act * (1.0 - gate_sigmoid))
    ).astype(jnp.bfloat16)
    up_grad = (mixed_grad * gate_silu).astype(jnp.bfloat16)
    gate_term = product_left(hidden_low, gate_grad)
    up_term = product_left(hidden_low, up_grad)
    hidden_part = product_right(gate_grad, gate_weight) + product_right(up_grad, up_weight)
    hidden_grad = upstream + lax.psum(hidden_part.astype(jnp.bfloat16), "tp").astype(jnp.float32)
    attn_gain_term = jnp.sum(hidden_grad * attn_sum * attn_scale, axis=0)
    attn_grad = norm_back(attn_sum, attn_scale, attention_gain, hidden_grad).astype(jnp.bfloat16)
    output_term = product_left(context_low, attn_grad)
    context_grad = (
        product_right(attn_grad, output_weight)
        .astype(jnp.bfloat16)
        .reshape(row_count, head_count, HD)
    )
    row_dot = jnp.transpose(jnp.sum(context_grad.astype(jnp.float32) * context, axis=-1))
    keys_all, values_all = (
        lax.all_gather(key_low, "ctx", axis=0, tiled=True),
        lax.all_gather(value_low, "ctx", axis=0, tiled=True),
    )
    block_rows = math.gcd(512, length)
    block_count = length // block_rows
    keys_blocks = keys_all.reshape(block_count, block_rows, head_count, HD)
    values_blocks = values_all.reshape(block_count, block_rows, head_count, HD)
    block_starts = jnp.arange(block_count, dtype=jnp.int32) * block_rows
    term_width = 2 * local_width

    def back_block(query_acc, block_in):
        keys_block, values_block, offset = block_in

        def back_compute(acc_now):
            scores = (
                jnp.einsum(
                    "qhd,khd->hqk", query_low, keys_block, preferred_element_type=jnp.float32
                )
                * score_scale
            )
            key_pos = offset + jnp.arange(block_rows, dtype=jnp.int32)
            visible = key_pos[None, :] <= positions[:, None]
            weights = jnp.where(visible[None], jnp.exp(scores - log_total[..., None]), 0.0)
            weight_grad = jnp.einsum(
                "qhd,khd->hqk", context_grad, values_block, preferred_element_type=jnp.float32
            )
            score_grad = (weights * (weight_grad - row_dot[..., None])).astype(jnp.bfloat16)
            acc_now = (
                acc_now
                + jnp.einsum(
                    "hqk,khd->qhd", score_grad, keys_block, preferred_element_type=jnp.float32
                )
                * score_scale
            )
            value_term = jnp.einsum(
                "hqk,qhd->khd",
                weights.astype(jnp.bfloat16),
                context_grad,
                preferred_element_type=jnp.float32,
            )
            key_term = (
                jnp.einsum(
                    "hqk,qhd->khd", score_grad, query_low, preferred_element_type=jnp.float32
                )
                * score_scale
            )
            joined = jnp.concatenate(
                [
                    key_term.reshape(block_rows, local_width),
                    value_term.reshape(block_rows, local_width),
                ],
                axis=-1,
            )
            return (acc_now, joined)

        def skipped(acc_now):
            return (acc_now, jnp.zeros((block_rows, term_width), jnp.float32))

        return lax.cond(offset <= last_row, back_compute, skipped, query_acc)

    query_acc, key_terms = lax.scan(
        back_block,
        jnp.zeros((row_count, head_count, HD), jnp.float32),
        (keys_blocks, values_blocks, block_starts),
    )
    key_value_grad = lax.psum_scatter(
        key_terms.reshape(length, 2 * local_width).astype(jnp.bfloat16),
        "ctx",
        scatter_dimension=0,
        tiled=True,
    ).astype(jnp.float32)
    key_rot_grad = key_value_grad[:, :local_width]
    value_grad = key_value_grad[:, local_width:].astype(jnp.bfloat16)
    query_normed_grad = rotate_back(query_acc, cosine_table, sine_table).reshape(
        row_count, local_width
    )
    key_normed_grad = rotate_back(
        key_rot_grad.reshape(row_count, head_count, HD), cosine_table, sine_table
    ).reshape(row_count, local_width)
    query_inner, key_inner = lax.psum(
        (
            jnp.sum(query_normed_grad * query_gain * query_raw, axis=1),
            jnp.sum(key_normed_grad * key_gain * key_raw, axis=1),
        ),
        "tp",
    )
    query_gain_term = jnp.sum(query_normed_grad * query_raw * query_scale, axis=0)
    key_gain_term = jnp.sum(key_normed_grad * key_raw * key_scale, axis=0)
    query_raw_grad = (
        query_scale * query_gain * query_normed_grad
        - query_raw * query_scale**3 * (query_inner / full_width)[:, None]
    ).astype(jnp.bfloat16)
    key_raw_grad = (
        key_scale * key_gain * key_normed_grad
        - key_raw * key_scale**3 * (key_inner / full_width)[:, None]
    ).astype(jnp.bfloat16)
    query_term = product_left(tokens, query_raw_grad)
    key_term_all = product_left(tokens, key_raw_grad)
    value_term_all = product_left(tokens, value_grad)
    tokens_part = (
        product_right(query_raw_grad, query_weight)
        + product_right(key_raw_grad, key_weight)
        + product_right(value_grad, value_weight)
    )
    tokens_grad = hidden_grad + lax.psum(tokens_part.astype(jnp.bfloat16), "tp").astype(jnp.float32)
    (
        query_weight_grad,
        key_weight_grad,
        value_weight_grad,
        output_weight_grad,
        gate_weight_grad,
        up_weight_grad,
        down_weight_grad,
    ) = (
        lax.psum_scatter(
            query_term.astype(jnp.bfloat16), "ctx", scatter_dimension=0, tiled=True
        ).astype(jnp.float32),
        lax.psum_scatter(
            key_term_all.astype(jnp.bfloat16), "ctx", scatter_dimension=0, tiled=True
        ).astype(jnp.float32),
        lax.psum_scatter(
            value_term_all.astype(jnp.bfloat16), "ctx", scatter_dimension=0, tiled=True
        ).astype(jnp.float32),
        lax.psum_scatter(
            output_term.astype(jnp.bfloat16), "ctx", scatter_dimension=1, tiled=True
        ).astype(jnp.float32),
        lax.psum_scatter(
            gate_term.astype(jnp.bfloat16), "ctx", scatter_dimension=0, tiled=True
        ).astype(jnp.float32),
        lax.psum_scatter(
            up_term.astype(jnp.bfloat16), "ctx", scatter_dimension=0, tiled=True
        ).astype(jnp.float32),
        lax.psum_scatter(
            down_term.astype(jnp.bfloat16), "ctx", scatter_dimension=1, tiled=True
        ).astype(jnp.float32),
    )
    query_gain_grad, key_gain_grad, attention_gain_grad, feedforward_gain_grad = lax.psum(
        (query_gain_term, key_gain_term, attn_gain_term, ffn_gain_term), "ctx"
    )
    return (
        layer_output.astype(jnp.bfloat16),
        tokens_grad,
        query_weight_grad,
        key_weight_grad,
        value_weight_grad,
        output_weight_grad,
        gate_weight_grad,
        up_weight_grad,
        down_weight_grad,
        query_gain_grad,
        key_gain_grad,
        attention_gain_grad,
        feedforward_gain_grad,
    )


def solution(mesh):
    in_specs = (
        P("ctx", None),
        P(None, "tp"),
        P(None, "tp"),
        P(None, "tp"),
        P("tp", None),
        P(None, "tp"),
        P(None, "tp"),
        P("tp", None),
        P("tp"),
        P("tp"),
        P(),
        P(),
        P("ctx", None),
    )
    out_specs = (
        P("ctx", None),
        P("ctx", None),
        P("ctx", "tp"),
        P("ctx", "tp"),
        P("ctx", "tp"),
        P("tp", "ctx"),
        P("ctx", "tp"),
        P("ctx", "tp"),
        P("tp", "ctx"),
        P("tp"),
        P("tp"),
        P(),
        P(),
    )
    return jax.shard_map(
        per_device, mesh=mesh, in_specs=in_specs, out_specs=out_specs, check_vma=False
    )
```

profile of v0, /device:TPU:0, one launch (start us, length us, event | category | flops | bytes accessed | tf_op | source)
XLA Modules:
  0.0 2292.9 jit_solution(10948310740585764582)
XLA Ops:
  13.9 7.0 all-reduce.2
  33.9 84.1 %all-gather.5.cloned.1.call-done = bf16[8192,512]{1,0:T(8,128)(2,1)} async-done(((bf16[256,512]{1,0:T(8,128)(2,1)}), bf16[8192,512]{1,0:T(8,128)(2,1)}) %all-gather.5.cloned.1.call-update) | async-done | bytes 8388624 | tf_op jit(solution)/shard_map/all_gather | solution.py:125
  118.0 107.7 %all-gather.3.cloned.1.call-done = bf16[8192,512]{0,1:T(8,128)(2,1)} async-done(((bf16[256,512]{0,1:T(8,128)(2,1)}), bf16[8192,512]{0,1:T(8,128)(2,1)}) %all-gather.3.cloned.1.call-update) | async-done | bytes 8388624 | tf_op jit(solution)/shard_map/all_gather | solution.py:124
  225.7 58.8 %conditional.2 = (f32[4,256]{1,0:T(4,128)}, f32[4,256]{1,0:T(4,128)}, f32[4,256]{1,0:T(4,128)S(1)}, f32[256,4,128]{0,2,1:T(8,128)}) conditional(s32[]{:T(128)} %convert_element_type.164, () %tuple.36, (s32[256]{0:T(256)S(1)}, bf16[8192,512]{0,1:T(8,128)(2,1)}, bf16[256,4,128]{0,2,1:T(8,128)(2,1)}, bf16[8192,512]{1,0:T(8,128)(2,1)}) %tuple.37), branch_computations={%region_4.0_spmd, %region_5.8_spmd} | conditional | flops 4406115328 | bytes 127697952 | solution.py:153
  228.3 17.2 fusion.2
  246.1 19.3 fusion.10
  265.4 16.4 fusion.4
  289.9 41.7 %all-reduce.8.cloned.1.call-done = bf16[256,2048]{1,0:T(8,128)(2,1)} async-done(((bf16[256,2048]{1,0:T(8,128)(2,1)}), bf16[256,2048]{1,0:T(8,128)(2,1)}) %all-reduce.8.cloned.1.call-update) | async-done | bytes 1048592 | tf_op jit(solution)/shard_map/psum | solution.py:159
  335.2 6.1 fusion.66
  350.0 42.2 %all-reduce.10.cloned.1.call-done = bf16[256,2048]{1,0:T(8,128)(2,1)} async-done(((bf16[256,2048]{1,0:T(8,128)(2,1)}), bf16[256,2048]{1,0:T(8,128)(2,1)}) %all-reduce.10.cloned.1.call-update) | async-done | bytes 1048592 | tf_op jit(solution)/shard_map/psum | solution.py:170
  396.0 7.8 multiply_convert_fusion
  406.3 6.8 fusion.35
  413.2 11.0 copy.137
  424.2 14.9 copy.88
  439.0 12.6 reshape.242
  451.6 8.9 copy.89
  471.2 86.0 %while.16 = (s32[]{:T(128)}, f32[256,4,128]{2,0,1:T(8,128)}, bf16[16,512,1024]{2,1,0:T(8,128)(2,1)}, s32[16]{0:T(128)S(1)}, s32[]{:T(128)}, /*index=5*/bf16[16,5...) while((s32[]{:T(128)}, f32[256,4,128]{2,0,1:T(8,128)}, ...), condition=%wide.region_19.20_spmd.clone, body=%wide.region_16.19_spmd.clone.sunk | while | flops 677774080 | bytes 29116772 | solution.py:258
  472.4 7.8 conditional.5
  561.8 7.5 convolution_convert_fusion
  569.6 7.2 convolution_convert_fusion.1
  576.9 7.2 convolution_convert_fusion.2
  586.2 312.5 %reduce-scatter.15.cloned.1.call-done = bf16[256,1024]{1,0:T(8,128)(2,1)} async-done(((bf16[8192,1024]{1,0:T(8,128)(2,1)}), bf16[256,1024]{1,0:T(8,128)(2,1)}) %reduce-scatter.15.cloned.1.call-update) | async-done | bytes 524304 | tf_op jit(solution)/shard_map/reduce_scatter | solution.py:263
  914.1 6.1 all-reduce.1
  946.2 3.9 copy.114
  950.1 135.6 %reduce-scatter.17.cloned.1.call-done = bf16[512,64]{0,1:T(8,128)(2,1)} async-done(((bf16[512,2048]{0,1:T(8,128)(2,1)}), bf16[512,64]{0,1:T(8,128)(2,1)}) %reduce-scatter.17.cloned.1.call-update) | async-done | bytes 65552 | tf_op jit(solution)/shard_map/reduce_scatter | solution.py:321
  1087.2 198.5 %reduce-scatter.23.cloned.1.call-done = bf16[2048,64]{0,1:T(8,128)(2,1)} async-done(((bf16[2048,2048]{0,1:T(8,128)(2,1)}), bf16[2048,64]{0,1:T(8,128)(2,1)}) %reduce-scatter.23.cloned.1.call-update) | async-done | bytes 262160 | tf_op jit(solution)/shard_map/reduce_scatter | solution.py:330
  1287.5 198.6 %reduce-scatter.21.cloned.1.call-done = bf16[64,2048]{1,0:T(8,128)(2,1)} async-done(((bf16[2048,2048]{1,0:T(8,128)(2,1)}), bf16[64,2048]{1,0:T(8,128)(2,1)}) %reduce-scatter.21.cloned.1.call-update) | async-done | bytes 262160 | tf_op jit(solution)/shard_map/reduce_scatter | solution.py:327
  1487.8 198.6 %reduce-scatter.19.cloned.1.call-done = bf16[64,2048]{1,0:T(8,128)(2,1)} async-done(((bf16[2048,2048]{1,0:T(8,128)(2,1)}), bf16[64,2048]{1,0:T(8,128)(2,1)}) %reduce-scatter.19.cloned.1.call-update) | async-done | bytes 262160 | tf_op jit(solution)/shard_map/reduce_scatter | solution.py:324
  1688.2 176.6 %all-reduce = (f32[512]{0:T(512)}, f32[512]{0:T(512)}, f32[2048]{0:T(1024)}, f32[2048]{0:T(1024)}) all-reduce(f32[512]{0:T(512)S(1)} %get-tuple-element.306, f32[512]{0:T(512)S(1)} %get-tuple-element.304, f32[2048]{0:T(1024)S(1)} %get-tuple-element.300, f32[2048]{0:T(1024)S(1)} %get-tuple-element.302), channel_id=1, replica_groups=mesh['ctx'=32,'tp'=4] {'ctx'}, use_global_device_ids=true, to_apply=%region_34.35 | all-reduce | flops 5120 | bytes 40960 | tf_op jit(solution)/shard_map/psum | solution.py:334
  1868.2 47.6 %reduce-scatter.27.cloned.1.call-done = bf16[64,512]{1,0:T(8,128)(2,1)} async-done(((bf16[2048,512]{1,0:T(8,128)(2,1)}), bf16[64,512]{1,0:T(8,128)(2,1)}) %reduce-scatter.27.cloned.1.call-update) | async-done | bytes 65552
  1917.6 182.6 %reduce-scatter.25.cloned.1.call-done = bf16[64,512]{1,0:T(8,128)(2,1)} async-done(((bf16[2048,512]{1,0:T(8,128)(2,1)}), bf16[64,512]{1,0:T(8,128)(2,1)}) %reduce-scatter.25.cloned.1.call-update) | async-done | bytes 65552
  2101.9 182.5 %reduce-scatter.29.cloned.1.call-done = bf16[64,512]{1,0:T(8,128)(2,1)} async-done(((bf16[2048,512]{1,0:T(8,128)(2,1)}), bf16[64,512]{1,0:T(8,128)(2,1)}) %reduce-scatter.29.cloned.1.call-update) | async-done | bytes 65552
  (337 shorter events, 199.4 us)
Async XLA Ops:
  7.2 110.8 %all-gather.5.cloned.1.call-start = ((), (), s32[]{:S(2)}) async-start(), calls=%async_computation.9 | async-start | bytes 8650752 | tf_op jit(solution)/shard_map/all_gather | solution.py:125
  10.7 215.0 %all-gather.3.cloned.1.call-start = ((), (), s32[]{:S(2)}) async-start(), calls=%async_computation.8 | async-start | bytes 8650752 | tf_op jit(solution)/shard_map/all_gather | solution.py:124
  12.4 9.7 copy-start.33
  12.4 13.7 copy-start.31
  21.5 8.5 copy-start.37
  33.1 298.5 %all-reduce.8.cloned.1.call-start = ((), (), s32[]{:S(2)}) async-start(), calls=%async_computation.10 | async-start | bytes 2097152 | tf_op jit(solution)/shard_map/psum | solution.py:159
  286.3 46.8 %copy-start.29 = (f32[2048]{0:T(1024)S(1)}, f32[2048]{0:T(1024)}, u32[]{:S(2)}) copy-start(f32[2048]{0:T(1024)} %param.29) | copy-start | bytes 24580
  289.7 102.6 %all-reduce.10.cloned.1.call-start = ((), (), s32[]{:S(2)}) async-start(), calls=%async_computation.11 | async-start | bytes 2097152 | tf_op jit(solution)/shard_map/psum | solution.py:170
  333.2 8.1 slice-start.4
  335.2 11.1 slice-start
  349.6 44.4 %copy-start.2 = (bf16[256,2048]{1,0:T(8,128)(2,1)S(1)}, bf16[256,2048]{1,0:T(8,128)(2,1)}, u32[]{:S(2)}) copy-start(bf16[256,2048]{1,0:T(8,128)(2,1)} %param.31) | copy-start | bytes 3145732
  349.6 44.4 %copy-start.30 = (f32[2048]{0:T(1024)S(1)}, f32[2048]{0:T(1024)}, u32[]{:S(2)}) copy-start(f32[2048]{0:T(1024)} %param.30) | copy-start | bytes 24580
  349.6 111.7 %all-reduce.12.cloned.1.call-start = ((), (), s32[]{:S(2)}) async-start(), calls=%async_computation.12 | async-start | bytes 2097152 | tf_op jit(solution)/shard_map/psum | solution.py:187
  392.2 11.6 slice-start.2
  396.0 7.9 slice-start.3
  413.1 485.6 %reduce-scatter.15.cloned.1.call-start = ((), (), s32[]{:S(2)}) async-start(), calls=%async_computation.13 | async-start | bytes 17301504 | tf_op jit(solution)/shard_map/reduce_scatter | solution.py:263
  557.2 528.5 %reduce-scatter.17.cloned.1.call-start = ((), (), s32[]{:S(2)}) async-start(), calls=%async_computation.15 | async-start | bytes 2162688 | tf_op jit(solution)/shard_map/reduce_scatter | solution.py:321
  560.6 725.1 %reduce-scatter.23.cloned.1.call-start = ((), (), s32[]{:S(2)}) async-start(), calls=%async_computation.18 | async-start | bytes 8650752 | tf_op jit(solution)/shard_map/reduce_scatter | solution.py:330
  569.4 916.7 %reduce-scatter.21.cloned.1.call-start = ((), (), s32[]{:S(2)}) async-start(), calls=%async_computation.17 | async-start | bytes 8650752 | tf_op jit(solution)/shard_map/reduce_scatter | solution.py:327
  576.8 1109.6 %reduce-scatter.19.cloned.1.call-start = ((), (), s32[]{:S(2)}) async-start(), calls=%async_computation.16 | async-start | bytes 8650752 | tf_op jit(solution)/shard_map/reduce_scatter | solution.py:324
  584.1 318.4 %copy-start.26 = (f32[256,64]{0,1:T(8,128)S(1)}, f32[256,64]{0,1:T(8,128)}, u32[]{:S(2)}) copy-start(f32[256,64]{0,1:T(8,128)} %copy-done.25) | copy-start | bytes 196612
  584.1 318.4 %copy-start.28 = (f32[256,64]{0,1:T(8,128)S(1)}, f32[256,64]{0,1:T(8,128)}, u32[]{:S(2)}) copy-start(f32[256,64]{0,1:T(8,128)} %copy-done.27) | copy-start | bytes 196612
  584.1 1280.8 %all-reduce.14.cloned.1.call-start = ((), (), s32[]{:S(2)}) async-start(), calls=%async_computation.14 | async-start | bytes 2097152 | tf_op jit(solution)/shard_map/psum | solution.py:302
  904.5 6.8 copy-start.34
  904.5 6.8 copy-start.36
  905.4 7.3 copy-start.32
  905.4 7.3 copy-start.38
  907.4 12.8 copy-start.40
  909.2 12.4 copy-start.39
  928.1 987.8 %reduce-scatter.27.cloned.1.call-start = ((), (), s32[]{:S(2)}) async-start(), calls=%async_computation.20 | async-start | bytes 2162688
  935.5 1164.7 %reduce-scatter.25.cloned.1.call-start = ((), (), s32[]{:S(2)}) async-start(), calls=%async_computation.19 | async-start | bytes 2162688
  942.8 1341.7 %reduce-scatter.29.cloned.1.call-start = ((), (), s32[]{:S(2)}) async-start(), calls=%async_computation.21 | async-start | bytes 2162688
  (45 other events, 85.1 us)
Sparse Core Ops, SparseCore 0:
  11.2 106.7 all-gather.4
  121.3 104.3 all-gather.2
  289.8 41.8 all-reduce.7
  349.7 42.4 all-reduce.9
  413.2 42.4 all-reduce.11
  557.3 341.2 reduce-scatter.14
  901.1 184.5 reduce-scatter.16
  1088.1 197.5 reduce-scatter.22
  1288.1 197.8 reduce-scatter.20
  1488.3 198.0 reduce-scatter.18
  1689.0 36.2 all-reduce.13
  1727.6 188.1 reduce-scatter.26
  1918.2 181.9 reduce-scatter.24
  2102.6 181.8 reduce-scatter.28
where the time goes:
time: 2300 us; the launch traced here: 2290 us
  waiting for transfers between devices  1730 us (75%)
  blocking collectives  190 us (8%)
  local copies, waits for them, and re-layouts  155 us (7%)
  matrix products  121 us (5%)
  other arithmetic  66.4 us (3%)
    unnamed x17, waiting for transfers between devices  413 us
    reduce_scatter x1, waiting for transfers between devices, per_device(): lax.psum_scatter(key_terms.reshape(length, 2 * local_width).astype(jnp.bf...  313 us
    reduce_scatter x1, waiting for transfers between devices, per_device(): lax.psum_scatter(gate_term.astype(jnp.bfloat16), 'ctx', scatter_dimension...  199 us
    reduce_scatter x1, waiting for transfers between devices, per_device(): lax.psum_scatter(up_term.astype(jnp.bfloat16), 'ctx', scatter_dimension=0...  199 us
    reduce_scatter x1, waiting for transfers between devices, per_device(): lax.psum_scatter(down_term.astype(jnp.bfloat16), 'ctx', scatter_dimension...  199 us
    psum x1, blocking collectives, per_device(): lax.psum((query_gain_term, key_gain_term, attn_gain_term, ffn_gain_term),...  177 us
    reduce_scatter x1, waiting for transfers between devices, per_device(): lax.psum_scatter(output_term.astype(jnp.bfloat16), 'ctx', scatter_dimensi...  136 us
    all_gather x1, waiting for transfers between devices, per_device(): remote_keys = lax.all_gather(key_low, 'ctx', axis=0, tiled=True)  108 us
  transfers between devices with their start and end apart: 14, of which 12 were waited for; matrix products, arithmetic and copies ran while one was open for 6% of the time, Pallas kernels for 0%

commit v1 on v0

v1 whole, which is shorter than its diff:
```python
import functools
import math

import jax
import jax.numpy as jnp
from jax import lax
from jax.experimental import pallas as pl
from jax.experimental.pallas import tpu as pltpu
from jax.sharding import Mesh
from jax.sharding import PartitionSpec as P

HD = 128
AXES = {"x": 4, "yh": 2, "z": 4, "yl": 2, "c": 2}
CTX = ("x", "yh", "z")
TP = ("yl", "c")
ROWS = 256
HALF = 128
HEADS = 4
EXTRA = 16
TILE = 1024

epsilon = 1e-06
rope_base = 500000.0
negative = -1e30
score_scale = 1.0 / math.sqrt(HD)


def product(left, right):
    return jnp.dot(left, right, preferred_element_type=jnp.float32)


def product_left(left, right):
    return lax.dot_general(
        left, right, (((0,), (0,)), ((), ())), preferred_element_type=jnp.float32
    )


def product_right(left, right):
    return lax.dot_general(
        left, right, (((1,), (1,)), ((), ())), preferred_element_type=jnp.float32
    )


def norm_back(values_in, scale_in, gain_in, grad_in):
    scaled_grad = grad_in * gain_in
    inner = jnp.mean(scaled_grad * values_in, axis=-1, keepdims=True)
    return scale_in * scaled_grad - values_in * scale_in**3 * inner


def exchange(values, axes):
    return lax.all_to_all(values, axes, split_axis=0, concat_axis=0, tiled=True)


def swap(values, axis):
    return lax.ppermute(values, axis, [(0, 1), (1, 0)])


def half_sum(part):
    theirs = swap(part[HALF:].astype(jnp.bfloat16), "c")
    mine = (part[:HALF] + theirs.astype(jnp.float32)).astype(jnp.bfloat16)
    far = swap(mine, "yl")
    return mine.astype(jnp.float32) + far.astype(jnp.float32)


def whole_rows(half):
    return jnp.concatenate([half, swap(half, "c")], axis=0)


def pass_x(values, step):
    return lax.ppermute(values, "x", [(i, (i + step) % 4) for i in range(4)])


def gather_x(half):
    near = jnp.concatenate([half] + [pass_x(half, step) for step in range(1, 4)], axis=0)
    return near, swap(near, "c")


def columns_x(x, *values):
    blocks = []
    for step in range(4):
        target = (x + step) % 4
        share = [
            lax.dynamic_slice_in_dim(v, target * (v.shape[1] // 4), v.shape[1] // 4, 1)
            for v in values
        ]
        share = share[0] if len(share) == 1 else jnp.concatenate(share, axis=1)
        blocks.append(pass_x(share, step) if step else share)
    return blocks


def weight_part(shared, blocks):
    near, far = shared
    total = product_left(near, jnp.concatenate([b[:HALF] for b in blocks], axis=0)) + product_left(
        far, jnp.concatenate([b[HALF:] for b in blocks], axis=0)
    )
    return total.astype(jnp.bfloat16)


def weight_sum(shared, blocks):
    part = weight_part(shared, blocks)
    rows, width = part.shape[0] // 32, part.shape[1]
    got = exchange(part.reshape(32, rows, width), CTX).reshape(4, 8, rows, width)
    return jnp.sum(got.astype(jnp.float32), axis=1)


def weight_scatter(shared, blocks):
    part = weight_part(shared, blocks)
    rows, width = part.shape[0] // 32, part.shape[1]
    part = jnp.swapaxes(part.reshape(4, 8, rows, width), 0, 1).reshape(32 * rows, width)
    return lax.psum_scatter(part, ("yh", "z"), scatter_dimension=0, tiled=True).reshape(
        4, rows, width
    )


def sum_pairs(values, names):
    for name in names:
        count = AXES[name]
        step = 1
        while step < count:
            values = values + lax.ppermute(values, name, [(i, i ^ step) for i in range(count)])
            step *= 2
    return values


def side_by_side(parts):
    return jnp.concatenate([parts[i] for i in range(parts.shape[0])], axis=1)


def turn_kernel(place_ref, q_ref, k_ref, v_ref, qs_ref, ks_ref, qg_ref, kg_ref, cos_ref, sin_ref, qo_ref, kvo_ref):
    def turned(values):
        return (values * cos_ref[...] + pltpu.roll(values, HD // 2, 1) * sin_ref[...]).astype(jnp.bfloat16)

    queries = turned(q_ref[...] * qs_ref[...] * qg_ref[...])
    keys = turned(k_ref[...] * ks_ref[...] * kg_ref[...])
    qo_ref[0] = queries
    for i in range(4):
        kvo_ref[0, i, 0] = keys
        kvo_ref[0, i, 1] = v_ref[...]


def turn(place, query_raw, key_raw, value_low, query_scale, key_scale, query_gain, key_gain, cosine, sine):
    block = pl.BlockSpec((ROWS, HD), lambda h, place: (0, h))
    column = pl.BlockSpec((ROWS, 1), lambda h, place: (0, 0))
    gain = pl.BlockSpec((1, HD), lambda h, place: (0, h))
    table = pl.BlockSpec((ROWS, HD), lambda h, place: (0, 0))
    return pl.pallas_call(
        turn_kernel,
        grid_spec=pltpu.PrefetchScalarGridSpec(
            num_scalar_prefetch=1,
            grid=(HEADS,),
            in_specs=[block, block, block, column, column, gain, gain, table, table],
            out_specs=[
                pl.BlockSpec((1, ROWS, HD), lambda h, place: ((h - place[0]) & 3, 0, 0)),
                pl.BlockSpec((1, 4, 2, ROWS, HD), lambda h, place: (h, 0, 0, 0, 0)),
            ],
        ),
        out_shape=[
            jax.ShapeDtypeStruct((4, ROWS, HD), jnp.bfloat16),
            jax.ShapeDtypeStruct((4, 4, 2, ROWS, HD), jnp.bfloat16),
        ],
        name="turn",
    )(place, query_raw, key_raw, value_low, query_scale, key_scale, query_gain, key_gain, cosine, sine)


def to_rows(values):
    rows = []
    for _ in range(3):
        high = values.astype(jnp.bfloat16).astype(jnp.float32)
        rows += [high[:, :HD], high[:, HD:]]
        values = values - high
    return rows


def row_block(rows):
    rows = rows + [jnp.zeros((1, HD), jnp.float32)] * (EXTRA - len(rows))
    return jnp.concatenate(rows, axis=0).astype(jnp.bfloat16)


def from_rows(block, at):
    block = block.astype(jnp.float32)
    sides = [
        block[at + i : at + i + 1] + block[at + i + 2 : at + i + 3] + block[at + i + 4 : at + i + 5]
        for i in range(2)
    ]
    return jnp.concatenate(sides, axis=1)


def where_block(b, place):
    return ((place[0] - (b & 3)) & 3) * 2 + (place[1] ^ (b >> 2))


def keep(place_ref):
    zone, core = place_ref[2], place_ref[3]
    key_row = lax.broadcasted_iota(jnp.int32, (TILE, ROWS), 0)
    query_row = lax.broadcasted_iota(jnp.int32, (TILE, ROWS), 1)
    flip = core * HALF
    key_pos = (key_row & ~(ROWS - 1)) | ((key_row & (ROWS - 1)) ^ flip)
    query_pos = zone * ROWS + (query_row ^ flip)
    return key_pos <= query_pos


def attend_kernel(place_ref, q_ref, kv_ref, out_ref, turned_ref, max_ref, total_ref, sum_ref):
    block = pl.program_id(0)
    column, side = (place_ref[0] - (block & 3)) & 3, place_ref[1] ^ (block >> 2)
    own_side = place_ref[1]

    @pl.when(block == 0)
    def _():
        for i in range(4):
            for j in range(4):
                turned_ref[i, :, j * ROWS : (j + 1) * ROWS] = jnp.transpose(kv_ref[i, j, 1])

    max_ref[...] = jnp.full_like(max_ref, negative)
    total_ref[...] = jnp.zeros_like(total_ref)
    sum_ref[...] = jnp.zeros_like(sum_ref)
    queries = q_ref[0]

    def tile(i, masked):
        keys = kv_ref[i, :, 0].reshape(TILE, HD)
        scores = product_right(keys, queries) * score_scale
        if masked:
            scores = jnp.where(keep(place_ref), scores, negative)
        old_max = max_ref[...]
        new_max = jnp.maximum(old_max, jnp.max(scores, axis=0, keepdims=True))
        weights = jnp.exp(scores - new_max)
        fade = jnp.exp(old_max - new_max)
        max_ref[...] = new_max
        total_ref[...] = total_ref[...] * fade + jnp.sum(weights, axis=0, keepdims=True)
        sum_ref[...] = sum_ref[...] * fade + product(turned_ref[i], weights.astype(jnp.bfloat16))

    @pl.loop(0, column + jnp.where(side > own_side, 1, 0))
    def _(i):
        tile(i, False)

    @pl.when(side == own_side)
    def _():
        tile(column, True)

    seen = total_ref[...] > 0.0
    safe = jnp.where(seen, total_ref[...], 1.0)
    out_ref[0, :ROWS] = jnp.transpose(sum_ref[...] / safe).astype(jnp.bfloat16)
    lse = jnp.where(seen, max_ref[...] + jnp.log(safe), negative)
    out_ref[0, ROWS:] = row_block(to_rows(lse))


def attend(place, queries, keys_values):
    return pl.pallas_call(
        attend_kernel,
        grid_spec=pltpu.PrefetchScalarGridSpec(
            num_scalar_prefetch=1,
            grid=(8,),
            in_specs=[
                pl.BlockSpec((1, ROWS, HD), lambda b, place: (b, 0, 0)),
                pl.BlockSpec((4, 4, 2, ROWS, HD), lambda b, place: (0, 0, 0, 0, 0)),
            ],
            out_specs=pl.BlockSpec(
                (1, ROWS + EXTRA, HD), lambda b, place: (where_block(b, place), 0, 0)
            ),
            scratch_shapes=[
                pltpu.VMEM((4, HD, TILE), jnp.bfloat16),
                pltpu.VMEM((1, ROWS), jnp.float32),
                pltpu.VMEM((1, ROWS), jnp.float32),
                pltpu.VMEM((HD, ROWS), jnp.float32),
            ],
        ),
        out_shape=jax.ShapeDtypeStruct((8, ROWS + EXTRA, HD), jnp.bfloat16),
        compiler_params=pltpu.CompilerParams(vmem_limit_bytes=40 * 2**20),
        name="attend",
    )(place, queries, keys_values)


def merge_kernel(part_ref, context_ref, low_ref, log_ref):
    lse = jnp.concatenate([from_rows(part_ref[0, i, ROWS:], 0) for i in range(2)], axis=0)
    most = jnp.max(lse, axis=0, keepdims=True)
    shares = jnp.exp(lse - most)
    total = jnp.sum(shares, axis=0, keepdims=True)
    shares = shares / total
    context = jnp.zeros((ROWS, HD), jnp.float32)
    for i in range(2):
        share = jnp.transpose(jnp.broadcast_to(shares[i : i + 1], (HD, ROWS)))
        context = context + share * part_ref[0, i, :ROWS].astype(jnp.float32)
    context_ref[...] = context
    low_ref[...] = context.astype(jnp.bfloat16)
    log_ref[0] = most + jnp.log(total)


def merge(parts):
    block = pl.BlockSpec((ROWS, HD), lambda h: (0, h))
    return pl.pallas_call(
        merge_kernel,
        grid=(HEADS,),
        in_specs=[pl.BlockSpec((1, 2, ROWS + EXTRA, HD), lambda h: (h, 0, 0, 0))],
        out_specs=[block, block, pl.BlockSpec((1, 1, ROWS), lambda h: (h, 0, 0))],
        out_shape=[
            jax.ShapeDtypeStruct((ROWS, HEADS * HD), jnp.float32),
            jax.ShapeDtypeStruct((ROWS, HEADS * HD), jnp.bfloat16),
            jax.ShapeDtypeStruct((HEADS, 1, ROWS), jnp.float32),
        ],
        name="merge",
    )(parts)


def spread_kernel(grad_ref, context_ref, log_ref, out_ref):
    grad = grad_ref[...]
    dots = jnp.transpose(grad.astype(jnp.float32) * context_ref[...])
    row_dot = jnp.sum(dots, axis=0, keepdims=True)
    rows = row_block(to_rows(log_ref[0]) + to_rows(row_dot))
    for i in range(2):
        out_ref[0, i, :ROWS] = grad
        out_ref[0, i, ROWS:] = rows


def spread(context_grad, context, log_total):
    block = pl.BlockSpec((ROWS, HD), lambda h: (0, h))
    return pl.pallas_call(
        spread_kernel,
        grid=(HEADS,),
        in_specs=[block, block, pl.BlockSpec((1, 1, ROWS), lambda h: (h, 0, 0))],
        out_specs=pl.BlockSpec((1, 2, ROWS + EXTRA, HD), lambda h: (h, 0, 0, 0)),
        out_shape=jax.ShapeDtypeStruct((4, 2, ROWS + EXTRA, HD), jnp.bfloat16),
        name="spread",
    )(context_grad, context, log_total)


def attend_back_kernel(
    place_ref, q_ref, grad_ref, kv_ref, dq_ref, dkv_ref, turned_ref, total_ref, query_ref
):
    block = pl.program_id(0)
    column, side = (place_ref[0] - (block & 3)) & 3, place_ref[1] ^ (block >> 2)
    own_side = place_ref[1]

    @pl.when(block == 0)
    def _():
        total_ref[...] = jnp.zeros_like(total_ref)
        for i in range(4):
            for j in range(4):
                turned_ref[i, :, j * ROWS : (j + 1) * ROWS] = jnp.transpose(kv_ref[i, j, 0])

    query_ref[...] = jnp.zeros_like(query_ref)
    queries = q_ref[0]
    grads = grad_ref[0, :ROWS]
    log_total = from_rows(grad_ref[0, ROWS:], 0)
    row_dot = from_rows(grad_ref[0, ROWS:], 6)

    def tile(i, masked):
        keys = kv_ref[i, :, 0].reshape(TILE, HD)
        values = kv_ref[i, :, 1].reshape(TILE, HD)
        scores = product_right(keys, queries) * score_scale - log_total
        if masked:
            scores = jnp.where(keep(place_ref), scores, negative)
        weights = jnp.exp(scores)
        weight_grad = product_right(values, grads)
        score_grad = (weights * (weight_grad - row_dot)).astype(jnp.bfloat16)
        total_ref[i, 1] += product(weights.astype(jnp.bfloat16), grads)
        total_ref[i, 0] += product(score_grad, queries)
        query_ref[...] += product(turned_ref[i], score_grad)

    @pl.loop(0, column + jnp.where(side > own_side, 1, 0))
    def _(i):
        tile(i, False)

    @pl.when(side == own_side)
    def _():
        tile(column, True)

    dq_ref[0] = jnp.transpose(query_ref[...] * score_scale).astype(jnp.bfloat16)

    @pl.when(block == 7)
    def _():
        for i in range(4):
            for j in range(4):
                rows = slice(j * ROWS, (j + 1) * ROWS)
                dkv_ref[i, j, 0] = (total_ref[i, 0, rows] * score_scale).astype(jnp.bfloat16)
                dkv_ref[i, j, 1] = total_ref[i, 1, rows].astype(jnp.bfloat16)


def attend_back(place, queries, grads, keys_values):
    whole = pl.BlockSpec((4, 4, 2, ROWS, HD), lambda b, place: (0, 0, 0, 0, 0))
    block = pl.BlockSpec((1, ROWS, HD), lambda b, place: (b, 0, 0))
    return pl.pallas_call(
        attend_back_kernel,
        grid_spec=pltpu.PrefetchScalarGridSpec(
            num_scalar_prefetch=1,
            grid=(8,),
            in_specs=[
                block,
                pl.BlockSpec(
                    (1, ROWS + EXTRA, HD), lambda b, place: (where_block(b, place), 0, 0)
                ),
                whole,
            ],
            out_specs=[block, whole],
            scratch_shapes=[
                pltpu.VMEM((4, HD, TILE), jnp.bfloat16),
                pltpu.VMEM((4, 2, TILE, HD), jnp.float32),
                pltpu.VMEM((HD, ROWS), jnp.float32),
            ],
        ),
        out_shape=[
            jax.ShapeDtypeStruct((8, ROWS, HD), jnp.bfloat16),
            jax.ShapeDtypeStruct((4, 4, 2, ROWS, HD), jnp.bfloat16),
        ],
        compiler_params=pltpu.CompilerParams(vmem_limit_bytes=48 * 2**20),
        name="attend_back",
    )(place, queries, grads, keys_values)


def turn_back_kernel(
    place_ref, dq_ref, dkv_ref, q_ref, k_ref, qg_ref, kg_ref, cos_ref, sin_ref, qo_ref, ko_ref, vo_ref, qi_ref, ki_ref
):
    def turned(values):
        return values * cos_ref[...] - pltpu.roll(values, HD // 2, 1) * sin_ref[...]

    head = pl.program_id(0)
    queries = dq_ref[0].astype(jnp.float32)
    keys = jnp.zeros((ROWS, HD), jnp.float32)
    values = jnp.zeros((ROWS, HD), jnp.float32)
    for i in range(4):
        keys = keys + dkv_ref[0, i, 0].astype(jnp.float32)
        values = values + dkv_ref[0, i, 1].astype(jnp.float32)
    queries, keys = turned(queries), turned(keys)
    qo_ref[...] = queries
    ko_ref[...] = keys
    vo_ref[...] = values.astype(jnp.bfloat16)

    @pl.when(head == 0)
    def _():
        qi_ref[...] = jnp.zeros_like(qi_ref)
        ki_ref[...] = jnp.zeros_like(ki_ref)

    qi_ref[...] += queries * qg_ref[...] * q_ref[...]
    ki_ref[...] += keys * kg_ref[...] * k_ref[...]


def turn_back(place, query_grad, key_value_grad, query_raw, key_raw, query_gain, key_gain, cosine, sine):
    block = pl.BlockSpec((ROWS, HD), lambda h, place: (0, h))
    gain = pl.BlockSpec((1, HD), lambda h, place: (0, h))
    table = pl.BlockSpec((ROWS, HD), lambda h, place: (0, 0))
    wide = (ROWS, HEADS * HD)
    return pl.pallas_call(
        turn_back_kernel,
        grid_spec=pltpu.PrefetchScalarGridSpec(
            num_scalar_prefetch=1,
            grid=(HEADS,),
            in_specs=[
                pl.BlockSpec((1, ROWS, HD), lambda h, place: ((h - place[0]) & 3, 0, 0)),
                pl.BlockSpec((1, 4, 2, ROWS, HD), lambda h, place: (h, 0, 0, 0, 0)),
                block,
                block,
                gain,
                gain,
                table,
                table,
            ],
            out_specs=[block, block, block, table, table],
        ),
        out_shape=[
            jax.ShapeDtypeStruct(wide, jnp.float32),
            jax.ShapeDtypeStruct(wide, jnp.float32),
            jax.ShapeDtypeStruct(wide, jnp.bfloat16),
            jax.ShapeDtypeStruct((ROWS, HD), jnp.float32),
            jax.ShapeDtypeStruct((ROWS, HD), jnp.float32),
        ],
        name="turn_back",
    )(place, query_grad, key_value_grad, query_raw, key_raw, query_gain, key_gain, cosine, sine)


def per_device(
    tokens,
    query_weight,
    key_weight,
    value_weight,
    output_weight,
    gate_weight,
    up_weight,
    down_weight,
    query_gain,
    key_gain,
    attention_gain,
    feedforward_gain,
    cotangent,
):
    full_width = tokens.shape[1]
    x, yh, z, core = (lax.axis_index(name) for name in ("x", "yh", "z", "c"))
    place = jnp.stack([x, yh, z, core]).astype(jnp.int32)

    def own_first(values):
        return jnp.where(core == 0, values, jnp.concatenate([values[HALF:], values[:HALF]], axis=0))

    def sum_rows(first, second):
        both = jnp.stack([own_first(first), own_first(second)])
        both = lax.psum(both, TP)
        return jnp.stack([own_first(both[0]), own_first(both[1])])

    def own_rows(values):
        return lax.dynamic_slice_in_dim(values, core * HALF, HALF, 0)

    def natural_rows(mine):
        theirs = swap(mine, "c")
        return jnp.where(
            core == 0,
            jnp.concatenate([mine, theirs], axis=0),
            jnp.concatenate([theirs, mine], axis=0),
        )

    positions = (8 * x + 4 * yh + z) * ROWS + (jnp.arange(ROWS, dtype=jnp.int32) ^ (core * HALF))
    half_size = HD // 2
    frequency = 1.0 / rope_base ** (jnp.arange(half_size, dtype=jnp.float32) * 2.0 / HD)
    angles = positions.astype(jnp.float32)[:, None] * frequency[None, :]
    cosine, sine = jnp.cos(angles), jnp.sin(angles)
    cosine_table = jnp.concatenate([cosine, cosine], axis=1)
    sine_table = jnp.concatenate([-sine, sine], axis=1)
    query_row_gain, key_row_gain = query_gain[None], key_gain[None]

    tokens_own = own_rows(tokens)
    tokens_first = own_first(tokens)
    query_raw = product(tokens_first, query_weight)
    key_raw = product(tokens_first, key_weight)
    value_low = product(tokens_first, value_weight).astype(jnp.bfloat16)
    squares = sum_rows(jnp.sum(query_raw * query_raw, axis=1), jnp.sum(key_raw * key_raw, axis=1))
    scales = lax.rsqrt(squares / full_width + epsilon)
    query_scale, key_scale = scales[0][:, None], scales[1][:, None]
    query_sent, key_value_sent = turn(
        place,
        query_raw,
        key_raw,
        value_low,
        query_scale,
        key_scale,
        query_row_gain,
        key_row_gain,
        cosine_table,
        sine_table,
    )
    queries = jnp.stack(
        [query_sent[0]] + [pass_x(query_sent[step], step) for step in range(1, 4)]
    )
    queries = jnp.concatenate([queries, swap(queries, "yh")], axis=0)
    keys_values = exchange(key_value_sent.reshape(16, 2, ROWS, HD), ("x", "z")).reshape(
        4, 4, 2, ROWS, HD
    )
    tokens_all = gather_x(tokens_own)
    part = exchange(attend(place, queries, keys_values), ("x", "yh"))
    context, context_low, log_total = merge(part.reshape(4, 2, ROWS + EXTRA, HD))
    context_columns = columns_x(x, context_low)

    attn_sum = half_sum(product(context_low, output_weight))
    attn_scale = lax.rsqrt(jnp.mean(attn_sum * attn_sum, axis=-1, keepdims=True) + epsilon)
    hidden = tokens_own.astype(jnp.float32) + attn_sum * attn_scale * attention_gain
    hidden_own = hidden.astype(jnp.bfloat16)
    hidden_low = whole_rows(hidden_own)
    hidden_all = gather_x(hidden_own)
    gate_act = product(hidden_low, gate_weight)
    up_act = product(hidden_low, up_weight)
    gate_sigmoid = jax.nn.sigmoid(gate_act)
    gate_silu = gate_act * gate_sigmoid
    mixed_low = (gate_silu * up_act).astype(jnp.bfloat16)
    mixed_columns = columns_x(x, mixed_low)

    ffn_sum = half_sum(product(mixed_low, down_weight))
    ffn_scale = lax.rsqrt(jnp.mean(ffn_sum * ffn_sum, axis=-1, keepdims=True) + epsilon)
    layer_output = natural_rows(
        (hidden + ffn_sum * ffn_scale * feedforward_gain).astype(jnp.bfloat16)
    )
    upstream = own_rows(cotangent).astype(jnp.float32)
    ffn_gain_term = jnp.sum(upstream * ffn_sum * ffn_scale, axis=0)
    ffn_grad_own = norm_back(ffn_sum, ffn_scale, feedforward_gain, upstream).astype(jnp.bfloat16)
    ffn_grad = whole_rows(ffn_grad_own)
    ffn_grad_all = gather_x(ffn_grad_own)
    mixed_grad = product_right(ffn_grad, down_weight)
    gate_grad = (
        mixed_grad * up_act * gate_sigmoid * (1.0 + gate_act * (1.0 - gate_sigmoid))
    ).astype(jnp.bfloat16)
    up_grad = (mixed_grad * gate_silu).astype(jnp.bfloat16)
    gate_up_columns = columns_x(x, gate_grad, up_grad)
    hidden_part = product_right(gate_grad, gate_weight) + product_right(up_grad, up_weight)
    hidden_grad = upstream + half_sum(hidden_part)
    attn_gain_term = jnp.sum(hidden_grad * attn_sum * attn_scale, axis=0)
    attn_grad_own = norm_back(attn_sum, attn_scale, attention_gain, hidden_grad).astype(
        jnp.bfloat16
    )
    attn_grad = whole_rows(attn_grad_own)
    attn_grad_all = gather_x(attn_grad_own)
    context_grad = product_right(attn_grad, output_weight).astype(jnp.bfloat16)
    grads = exchange(
        spread(context_grad, context, log_total).reshape(8, ROWS + EXTRA, HD), ("x", "yh")
    )

    down_weight_part = weight_scatter(ffn_grad_all, mixed_columns)
    gate_up_weight_part = weight_scatter(hidden_all, gate_up_columns)
    output_weight_part = weight_scatter(attn_grad_all, context_columns)

    query_back, key_value_back = attend_back(place, queries, grads, keys_values)
    query_back = (
        query_back[:4].astype(jnp.float32) + swap(query_back[4:], "yh").astype(jnp.float32)
    ).astype(jnp.bfloat16)
    query_back = jnp.stack(
        [query_back[0]] + [pass_x(query_back[step], -step) for step in range(1, 4)]
    )
    key_value_back = exchange(key_value_back.reshape(16, 2, ROWS, HD), ("x", "z")).reshape(
        4, 4, 2, ROWS, HD
    )
    query_normed_grad, key_normed_grad, value_grad, query_inner, key_inner = turn_back(
        place,
        query_back,
        key_value_back,
        query_raw,
        key_raw,
        query_row_gain,
        key_row_gain,
        cosine_table,
        sine_table,
    )
    inner = sum_rows(jnp.sum(query_inner, axis=1), jnp.sum(key_inner, axis=1)) / full_width
    query_raw_grad = (
        query_scale * query_gain * query_normed_grad
        - query_raw * query_scale**3 * inner[0][:, None]
    ).astype(jnp.bfloat16)
    key_raw_grad = (
        key_scale * key_gain * key_normed_grad - key_raw * key_scale**3 * inner[1][:, None]
    ).astype(jnp.bfloat16)
    low_columns = columns_x(x, query_raw_grad, key_raw_grad, value_grad)
    tokens_part = (
        product_right(query_raw_grad, query_weight)
        + product_right(key_raw_grad, key_weight)
        + product_right(value_grad, value_weight)
    )
    tokens_grad = natural_rows(hidden_grad + half_sum(tokens_part))
    low_weight_grad = weight_sum(tokens_all, low_columns)
    late_weight_grad = exchange(
        jnp.concatenate([gate_up_weight_part, down_weight_part, output_weight_part], axis=2), "x"
    ).astype(jnp.float32)

    gains = sum_pairs(
        jnp.concatenate(
            [
                jnp.sum(query_normed_grad * query_raw * query_scale, axis=0),
                jnp.sum(key_normed_grad * key_raw * key_scale, axis=0),
                sum_pairs(jnp.concatenate([attn_gain_term, ffn_gain_term]), ("c",)),
            ]
        ),
        CTX,
    )
    return (
        layer_output,
        tokens_grad,
        side_by_side(low_weight_grad[:, :, 0:128]),
        side_by_side(low_weight_grad[:, :, 128:256]),
        side_by_side(low_weight_grad[:, :, 256:384]),
        jnp.transpose(side_by_side(late_weight_grad[:, :, 1536:1664])),
        side_by_side(late_weight_grad[:, :, 0:512]),
        side_by_side(late_weight_grad[:, :, 512:1024]),
        jnp.transpose(side_by_side(late_weight_grad[:, :, 1024:1536])),
        gains[0:512],
        gains[512:1024],
        gains[1024:3072],
        gains[3072:5120],
    )


def solution(mesh):
    chips = Mesh(mesh.devices.reshape(tuple(AXES.values())), tuple(AXES))
    in_specs = (
        P(CTX, None),
        P(None, TP),
        P(None, TP),
        P(None, TP),
        P(TP, None),
        P(None, TP),
        P(None, TP),
        P(TP, None),
        P(TP),
        P(TP),
        P(),
        P(),
        P(CTX, None),
    )
    out_specs = (
        P(CTX, None),
        P(CTX, None),
        P(CTX, TP),
        P(CTX, TP),
        P(CTX, TP),
        P(TP, CTX),
        P(CTX, TP),
        P(CTX, TP),
        P(TP, CTX),
        P(TP),
        P(TP),
        P(),
        P(),
    )
    return jax.shard_map(
        per_device, mesh=chips, in_specs=in_specs, out_specs=out_specs, check_vma=False
    )
```

time: 2300 us -> 593 us (0.26)
  waiting for transfers between devices: 1730 us -> 237 us
  blocking collectives: 190 us -> 26.9 us
  local copies, waits for them, and re-layouts: 155 us -> 26.4 us
  starting transfers between devices: 1.41 us -> 108 us
  matrix products: 121 us -> 62.3 us
  Pallas kernels: 0 us -> 56.4 us
    reduce_scatter x5 -> x3, waiting for transfers between devices: 1040 us -> 11.6 us  [weight_scatter(): lax.psum_scatter(part, ('yh', 'z'), scatter_dimension=0, tiled=True)]
    unnamed x17 -> x3, waiting for transfers between devices: 413 us -> 0.05 us
    ppermute x0 -> x55, waiting for transfers between devices: none -> 214 us  [the longest x30 119 us: pass_x(): return lax.ppermute(values, 'x', [(i, (i + step) % 4) for i in range(4)])]
    all_gather x2 -> x0, waiting for transfers between devices: 192 us -> none  [the longest x1 108 us: per_device(): remote_keys = lax.all_gather(key_low, 'ctx', axis=0, tiled=True)]
    psum x3 -> x2, blocking collectives: 190 us -> 13.1 us  [sum_rows(): both = lax.psum(both, TP)]
    psum x4 -> x0, waiting for transfers between devices: 83.9 us -> none  [the longest x1 42.2 us: per_device(): lax.psum(product(mixed_low, down_weight).astype(jnp.bfloat16), 'tp')]
    ppermute x0 -> x55, starting transfers between devices: none -> 80.5 us  [the longest x30 57.5 us: pass_x(): return lax.ppermute(values, 'x', [(i, (i + step) % 4) for i in range(4)])]
    pallas_call x0 -> x6, Pallas kernels: none -> 56.4 us  [the longest x1 20.2 us: attend_back(): pl.pallas_call(attend_back_kernel, grid_spec=pltpu.PrefetchScalarGridSpec...]
  transfers between devices with their start and end apart: 14 -> 63, of which waited for: 12 -> 34; matrix products, arithmetic and copies ran while one was open for 6% -> 12% of each run, Pallas kernels for 0% -> 5%
where the time goes in v1:
time: 593 us; the launch traced here: 584 us
  waiting for transfers between devices  237 us (40%)
  starting transfers between devices  108 us (18%)
  matrix products  62.3 us (11%)
  Pallas kernels  56.4 us (10%)
  other arithmetic  51.2 us (9%)
  blocking collectives  26.9 us (5%)
  local copies, waits for them, and re-layouts  26.4 us (4%)
  between operations  15.7 us (3%)
    ppermute x30, waiting for transfers between devices, pass_x(): return lax.ppermute(values, 'x', [(i, (i + step) % 4) for i in range(4)])  119 us
    ppermute x30, starting transfers between devices, pass_x(): return lax.ppermute(values, 'x', [(i, (i + step) % 4) for i in range(4)])  57.5 us
    ppermute x19, waiting for transfers between devices, swap(): return lax.ppermute(values, axis, [(0, 1), (1, 0)])  54.1 us
    ppermute x6, waiting for transfers between devices, sum_pairs(): lax.ppermute(values, name, [(i, i ^ step) for i in range(count)])  40.9 us
    all_to_all x5, starting transfers between devices, exchange(): return lax.all_to_all(values, axes, split_axis=0, concat_axis=0, tiled=True)  27.9 us
    dot_general x8, matrix products, product_left(): lax.dot_general(left, right, (((0,), (0,)), ((), ())), preferred_element_...  23.2 us
    pallas_call x1, Pallas kernels, attend_back(): pl.pallas_call(attend_back_kernel, grid_spec=pltpu.PrefetchScalarGridSpec...  20.2 us
    dot_general x7, matrix products, product_right(): lax.dot_general(left, right, (((1,), (1,)), ((), ())), preferred_element_...  19.9 us
  transfers between devices with their start and end apart: 63, of which 34 were waited for; matrix products, arithmetic and copies ran while one was open for 12% of the time, Pallas kernels for 5%

profile of v1, /device:TPU:0, one launch (start us, length us, event | category | flops | bytes accessed | tf_op | source)
XLA Modules:
  0.0 584.4 jit_solution(4442769467984291617)
XLA Ops:
  16.0 7.1 %psum.14 = f32[2,256]{1,0:T(2,128)S(1)} all-reduce(f32[2,256]{1,0:T(2,128)S(1)} %pad_maximum_fusion.27), channel_id=1, replica_groups=mesh['x'=4,'yh'=2,'z'=4,'yl'=2,'c'=2] {'yl','c'}, use_global_device_ids=true, to_apply=%region_2.3 | all-reduce | flops 512 | bytes 4096 | tf_op jit(solution)/shard_map/psum | solution.py:492
  28.0 5.2 turn.1
  33.2 8.1 %all-to-all-start = ((bf16[16,2,256,128]{3,2,1,0:T(8,128)(2,1)}), bf16[16,2,256,128]{3,2,1,0:T(8,128)(2,1)}, u32[]{:S(2)}, u32[]{:S(2)}) async-start(bf16[16,2,256,128]{3,2,1,0:T(8,128)(2,1)} %bitcast.174), calls=%async_computation | async-start | bytes 4194304 | tf_op jit(solution)/shard_map/all_to_all | solution.py:51
  47.4 20.7 %collective-permute-done = bf16[256,128]{1,0:T(8,128)(2,1)S(1)} collective-permute-done((bf16[256,128]{1,0:T(8,128)(2,1)S(1)}, bf16[256,128]{1,0:T(8,128)(2,1)S(1)}, u32[]{:S(2)}, u32[]{:S(2)}) %collective-permute-start) | collective-permute-done | bytes 65568 | tf_op jit(solution)/shard_map/ppermute | solution.py:70
  72.4 4.6 collective-permute-done.3
  77.0 18.7 %attend.1 = bf16[8,272,128]{2,1,0:T(8,128)(2,1)S(1)} custom-call(s32[4]{0:T(128)S(1)} %copy-done.4, bf16[8,256,128]{2,1,0:T(8,128)(2,1)S(1)} %constant_dynamic-update-slice_fusion.q_ref, bf16[4,4,2,256,128]{4,3,2,1,0:T(8,128)(2,1)} %bitcast.21.kv_ref), custom_call_target="tpu_custom_call" | custom-call | tf_op jit(solution)/shard_map/attend/pallas_call | solution.py:247
  95.7 13.8 %all_to_all.30 = bf16[8,272,128]{2,1,0:T(8,128)(2,1)} all-to-all(bf16[8,272,128]{2,1,0:T(8,128)(2,1)S(1)} %attend.1), channel_id=1, replica_groups=mesh['x'=4,'yh'=2,'z'=4,'yl'=2,'c'=2] {'x','yh'}, dimensions={0} | all-to-all | bytes 1114112 | tf_op jit(solution)/shard_map/all_to_all | solution.py:51
  119.9 12.3 %collective-permute-done.5 = bf16[128,2048]{1,0:T(8,128)(2,1)} collective-permute-done((bf16[128,2048]{1,0:T(8,128)(2,1)S(1)}, bf16[128,2048]{1,0:T(8,128)(2,1)}, u32[]{:S(2)}, u32[]{:S(2)}) %collective-permute-start.5) | collective-permute-done | bytes 524320 | tf_op jit(solution)/shard_map/ppermute | solution.py:55
  138.2 6.2 %fusion.37 = f32[256,2048]{1,0:T(8,128)S(1)} fusion(bf16[2048,2048]{1,0:T(8,128)(2,1)} %param.18, bf16[128,2048]{1,0:T(8,128)(2,1)S(1)} %collective-permute-done.6, bf16[128,2048]{1,0:T(8,128)(2,1)} %get-tuple-element.41), kind=kOutput, calls=%fused_computation.81 | convolution fusion | flops 2149580800 | bytes 11534336 | tf_op jit(solution)/shard_map/dot_general | solution.py:29
  155.6 12.2 %collective-permute-done.8 = bf16[128,2048]{1,0:T(8,128)(2,1)S(1)} collective-permute-done((bf16[128,2048]{1,0:T(8,128)(2,1)S(1)}, bf16[128,2048]{1,0:T(8,128)(2,1)S(1)}, u32[]{:S(2)}, u32[]{:S(2)}) %collective-permute-start.8) | collective-permute-done | bytes 524320 | tf_op jit(solution)/shard_map/ppermute | solution.py:55
  176.2 6.5 %fusion.126 = f32[256,2048]{1,0:T(8,128)S(1)} fusion(bf16[256,2048]{1,0:T(8,128)(2,1)S(1)} %get-tuple-element.44, bf16[2048,2048]{1,0:T(8,128)(2,1)} %param.18), kind=kOutput, calls=%fused_computation.302 | convolution fusion | flops 2147483648 | bytes 11534336 | tf_op jit(solution)/shard_map/dot_general | solution.py:39
  182.7 5.7 convolution_add_fusion.2
  192.5 12.2 %collective-permute-done.12 = bf16[128,2048]{1,0:T(8,128)(2,1)S(1)} collective-permute-done((bf16[128,2048]{1,0:T(8,128)(2,1)S(1)}, bf16[128,2048]{1,0:T(8,128)(2,1)S(1)}, u32[]{:S(2)}, u32[]{:S(2)}) %collective-permute-start.12) | collective-permute-done | bytes 524320 | tf_op jit(solution)/shard_map/ppermute | solution.py:55
  216.8 17.2 %collective-permute-done.44 = bf16[128,2048]{1,0:T(8,128)(2,1)S(1)} collective-permute-done((bf16[128,2048]{1,0:T(8,128)(2,1)S(1)}, bf16[128,2048]{1,0:T(8,128)(2,1)S(1)}, u32[]{:S(2)}, u32[]{:S(2)}) %collective-permute-start.44) | collective-permute-done | bytes 524320 | tf_op jit(solution)/shard_map/ppermute | solution.py:70
  241.5 13.4 %collective-permute-done.37 = bf16[128,2048]{1,0:T(8,128)(2,1)} collective-permute-done((bf16[128,2048]{1,0:T(8,128)(2,1)}, bf16[128,2048]{1,0:T(8,128)(2,1)}, u32[]{:S(2)}, u32[]{:S(2)}) %collective-permute-start.37) | collective-permute-done | bytes 524320 | tf_op jit(solution)/shard_map/ppermute | solution.py:70
  276.3 15.0 %collective-permute-start.28 = (bf16[128,2048]{1,0:T(8,128)(2,1)}, bf16[128,2048]{1,0:T(8,128)(2,1)}, u32[]{:S(2)}, u32[]{:S(2)}) collective-permute-start(bf16[128,2048]{1,0:T(8,128)(2,1)} %get-tuple-element.41), channel_id=1, source_target_pairs={{0,32},{32,64},{64,96},{96,0},{1,33},{33,65},{65,97},{97,1},{2,34}... | collective-permute-start | bytes 1572872 | tf_op jit(solution)/shard_map/ppermute | solution.py:70
  296.3 13.6 %collective-permute-done.38 = bf16[256,512]{1,0:T(8,128)(2,1)} collective-permute-done((bf16[256,512]{1,0:T(8,128)(2,1)S(1)}, bf16[256,512]{1,0:T(8,128)(2,1)}, u32[]{:S(2)}, u32[]{:S(2)}) %collective-permute-start.38) | collective-permute-done | bytes 262176 | tf_op jit(solution)/shard_map/ppermute | solution.py:70
  328.9 14.0 %collective-permute-done.23 = bf16[128,2048]{1,0:T(8,128)(2,1)S(1)} collective-permute-done((bf16[128,2048]{1,0:T(8,128)(2,1)S(1)}, bf16[128,2048]{1,0:T(8,128)(2,1)S(1)}, u32[]{:S(2)}, u32[]{:S(2)}) %collective-permute-start.23) | collective-permute-done | bytes 524320 | tf_op jit(solution)/shard_map/ppermute | solution.py:70
  351.4 4.5 collective-permute-done.33
  361.8 6.0 %all-to-all-start.2 = ((bf16[8,272,128]{2,1,0:T(8,128)(2,1)}), bf16[8,272,128]{2,1,0:T(8,128)(2,1)S(1)}, u32[]{:S(2)}, u32[]{:S(2)}) async-start(bf16[8,272,128]{2,1,0:T(8,128)(2,1)} %bitcast.172), calls=%async_computation.2 | async-start | bytes 1114112 | tf_op jit(solution)/shard_map/all_to_all | solution.py:51
  369.7 6.3 %collective-permute-done.31 = bf16[256,1024]{1,0:T(8,128)(2,1)} collective-permute-done((bf16[256,1024]{1,0:T(8,128)(2,1)}, bf16[256,1024]{1,0:T(8,128)(2,1)}, u32[]{:S(2)}, u32[]{:S(2)}) %collective-permute-start.31) | collective-permute-done | bytes 524320 | tf_op jit(solution)/shard_map/ppermute | solution.py:70
  381.8 20.2 %attend_back.1 = (bf16[8,256,128]{2,1,0:T(8,128)(2,1)S(1)}, bf16[4,4,2,256,128]{4,3,2,1,0:T(8,128)(2,1)S(1)}) custom-call(s32[4]{0:T(128)S(1)} %copy-done.4, bf16[8,256,128]{2,1,0:T(8,128)(2,1)S(1)} %constant_dynamic-update-slice_fusion.q_ref, bf16[8,272,128]{2,1,0:T(8,128)(2,1)S(1)} %all-to-all-done.2.grad_ref, bf16[4,4,2,256,128]{4,3,2,1,0:T(8,128)(2,1)} %bitcast.21.kv_ref), custom_call_target="tpu_custom_call" | custom-call | tf_op jit(solution)/shard_map/attend_back/pallas_call | solution.py:380
  404.1 4.7 all-to-all-start.3
  429.4 8.0 %collective-permute-done.17 = bf16[256,128]{1,0:T(8,128)(2,1)S(1)} collective-permute-done((bf16[256,128]{1,0:T(8,128)(2,1)S(1)}, bf16[256,128]{1,0:T(8,128)(2,1)S(1)}, u32[]{:S(2)}, u32[]{:S(2)}) %collective-permute-start.17) | collective-permute-done | bytes 65568 | tf_op jit(solution)/shard_map/ppermute | solution.py:70
  439.8 5.4 turn_back.1
  447.3 6.0 %psum.15 = f32[2,256]{1,0:T(2,128)S(1)} all-reduce(f32[2,256]{1,0:T(2,128)S(1)} %pad_maximum_fusion.28), channel_id=1, replica_groups=mesh['x'=4,'yh'=2,'z'=4,'yl'=2,'c'=2] {'yl','c'}, use_global_device_ids=true, to_apply=%region_9.10 | all-reduce | flops 512 | bytes 4096 | tf_op jit(solution)/shard_map/psum | solution.py:492
  462.6 5.5 collective-permute-done.50
  470.4 7.0 %collective-permute-done.25 = bf16[256,384]{1,0:T(8,128)(2,1)S(1)} collective-permute-done((bf16[256,384]{1,0:T(8,128)(2,1)S(1)}, bf16[256,384]{1,0:T(8,128)(2,1)S(1)}, u32[]{:S(2)}, u32[]{:S(2)}) %collective-permute-start.25) | collective-permute-done | bytes 196640 | tf_op jit(solution)/shard_map/ppermute | solution.py:70
  486.3 4.9 all-to-all-start.4
  497.5 32.3 %collective-permute-done.52 = f32[5120]{0:T(1024)S(1)} collective-permute-done((f32[5120]{0:T(1024)S(1)}, f32[5120]{0:T(1024)S(1)}, u32[]{:S(2)}, u32[]{:S(2)}) %collective-permute-start.52) | collective-permute-done | bytes 20512 | tf_op jit(solution)/shard_map/ppermute | solution.py:120
  542.4 11.6 %reduce-scatter.4.cloned.1.call-done = bf16[256,1024]{1,0:T(8,128)(2,1)} async-done(((bf16[2048,1024]{1,0:T(8,128)(2,1)}), bf16[256,1024]{1,0:T(8,128)(2,1)}) %reduce-scatter.4.cloned.1.call-update) | async-done | bytes 524304 | tf_op jit(solution)/shard_map/reduce_scatter | solution.py:110
  565.6 7.2 %all-to-all-done.5 = bf16[4,64,1664]{2,1,0:T(8,128)(2,1)} async-done(((bf16[4,64,1664]{2,1,0:T(8,128)(2,1)}), bf16[4,64,1664]{2,1,0:T(8,128)(2,1)}, u32[]{:S(2)}, u32[]{:S(2)}) %all-to-all-start.5) | async-done | bytes 852000 | tf_op jit(solution)/shard_map/all_to_all | solution.py:51
  (390 shorter events, 232.7 us)
Async XLA Ops:
  33.2 43.9 %all-to-all-start = ((bf16[16,2,256,128]{3,2,1,0:T(8,128)(2,1)}), bf16[16,2,256,128]{3,2,1,0:T(8,128)(2,1)}, u32[]{:S(2)}, u32[]{:S(2)}) async-start(bf16[16,2,256,128]{3,2,1,0:T(8,128)(2,1)} %bitcast.174), calls=%async_computation | async-start | bytes 4194304 | tf_op jit(solution)/shard_map/all_to_all | solution.py:51
  41.2 501.1 %reduce-scatter.8.cloned.1.call-start = ((), (), s32[]{:S(2)}) async-start(), calls=%async_computation.11 | async-start | bytes 589824 | tf_op jit(solution)/shard_map/reduce_scatter | solution.py:110
  41.3 26.7 %collective-permute-start = (bf16[256,128]{1,0:T(8,128)(2,1)S(1)}, bf16[256,128]{1,0:T(8,128)(2,1)S(1)}, u32[]{:S(2)}, u32[]{:S(2)}) collective-permute-start(bf16[256,128]{1,0:T(8,128)(2,1)S(1)} %get-tuple-element.131), channel_id=1, source_target_pairs={{0,32},{32,64},{64,96},{96,0},{1,33},{33,65},{65,97},{97,1},{2,34}... | collective-permute-start | bytes 196616 | tf_op jit(solution)/shard_map/ppermute | solution.py:70
  43.3 25.7 %collective-permute-start.1 = (bf16[256,128]{1,0:T(8,128)(2,1)S(1)}, bf16[256,128]{1,0:T(8,128)(2,1)S(1)}, u32[]{:S(2)}, u32[]{:S(2)}) collective-permute-start(bf16[256,128]{1,0:T(8,128)(2,1)S(1)} %get-tuple-element.130), channel_id=1, source_target_pairs={{0,64},{32,96},{64,0},{96,32},{1,65},{33,97},{65,1},{97,33},{2,66}... | collective-permute-start | bytes 196616 | tf_op jit(solution)/shard_map/ppermute | solution.py:70
  46.0 23.0 %collective-permute-start.2 = (bf16[256,128]{1,0:T(8,128)(2,1)S(1)}, bf16[256,128]{1,0:T(8,128)(2,1)S(1)}, u32[]{:S(2)}, u32[]{:S(2)}) collective-permute-start(bf16[256,128]{1,0:T(8,128)(2,1)S(1)} %get-tuple-element.129), channel_id=1, source_target_pairs={{0,96},{32,0},{64,32},{96,64},{1,97},{33,1},{65,33},{97,65},{2,98}... | collective-permute-start | bytes 196616 | tf_op jit(solution)/shard_map/ppermute | solution.py:70
  210.0 24.0 %collective-permute-start.44 = (bf16[128,2048]{1,0:T(8,128)(2,1)S(1)}, bf16[128,2048]{1,0:T(8,128)(2,1)S(1)}, u32[]{:S(2)}, u32[]{:S(2)}) collective-permute-start(bf16[128,2048]{1,0:T(8,128)(2,1)S(1)} %get-tuple-element.61), channel_id=1, source_target_pairs={{0,96},{32,0},{64,32},{96,64},{1,97},{33,1},{65,33},{97,65},{2,98}... | collective-permute-start | bytes 1572872 | tf_op jit(solution)/shard_map/ppermute | solution.py:70
  211.2 25.4 %collective-permute-start.43 = (bf16[128,2048]{1,0:T(8,128)(2,1)S(1)}, bf16[128,2048]{1,0:T(8,128)(2,1)S(1)}, u32[]{:S(2)}, u32[]{:S(2)}) collective-permute-start(bf16[128,2048]{1,0:T(8,128)(2,1)S(1)} %get-tuple-element.61), channel_id=1, source_target_pairs={{0,64},{32,96},{64,0},{96,32},{1,65},{33,97},{65,1},{97,33},{2,66}... | collective-permute-start | bytes 1572872 | tf_op jit(solution)/shard_map/ppermute | solution.py:70
  212.7 26.2 %collective-permute-start.42 = (bf16[128,2048]{1,0:T(8,128)(2,1)S(1)}, bf16[128,2048]{1,0:T(8,128)(2,1)S(1)}, u32[]{:S(2)}, u32[]{:S(2)}) collective-permute-start(bf16[128,2048]{1,0:T(8,128)(2,1)S(1)} %get-tuple-element.61), channel_id=1, source_target_pairs={{0,32},{32,64},{64,96},{96,0},{1,33},{33,65},{65,97},{97,1},{2,34}... | collective-permute-start | bytes 1572872 | tf_op jit(solution)/shard_map/ppermute | solution.py:70
  212.7 42.1 %collective-permute-start.37 = (bf16[128,2048]{1,0:T(8,128)(2,1)}, bf16[128,2048]{1,0:T(8,128)(2,1)}, u32[]{:S(2)}, u32[]{:S(2)}) collective-permute-start(bf16[128,2048]{1,0:T(8,128)(2,1)} %fusion.5), channel_id=1, source_target_pairs={{0,96},{32,0},{64,32},{96,64},{1,97},{33,1},{65,33},{97,65},{2,98}... | collective-permute-start | bytes 1572872 | tf_op jit(solution)/shard_map/ppermute | solution.py:70
  215.9 40.6 %collective-permute-start.36 = (bf16[128,2048]{1,0:T(8,128)(2,1)}, bf16[128,2048]{1,0:T(8,128)(2,1)}, u32[]{:S(2)}, u32[]{:S(2)}) collective-permute-start(bf16[128,2048]{1,0:T(8,128)(2,1)} %fusion.5), channel_id=1, source_target_pairs={{0,64},{32,96},{64,0},{96,32},{1,65},{33,97},{65,1},{97,33},{2,66}... | collective-permute-start | bytes 1572872 | tf_op jit(solution)/shard_map/ppermute | solution.py:70
  234.0 26.6 %collective-permute-start.35 = (bf16[128,2048]{1,0:T(8,128)(2,1)}, bf16[128,2048]{1,0:T(8,128)(2,1)}, u32[]{:S(2)}, u32[]{:S(2)}) collective-permute-start(bf16[128,2048]{1,0:T(8,128)(2,1)} %fusion.5), channel_id=1, source_target_pairs={{0,32},{32,64},{64,96},{96,0},{1,33},{33,65},{65,97},{97,1},{2,34}... | collective-permute-start | bytes 1572872 | tf_op jit(solution)/shard_map/ppermute | solution.py:70
  240.5 51.6 %collective-permute-start.48 = (bf16[512,2048]{1,0:T(8,128)(2,1)}, bf16[512,2048]{1,0:T(8,128)(2,1)}, u32[]{:S(2)}, u32[]{:S(2)}) collective-permute-start(bf16[512,2048]{1,0:T(8,128)(2,1)} %pad_maximum_fusion.3), channel_id=1, source_target_pairs={{0,1},{1,0},{2,3},{3,2},{4,5},{5,4},{6,7},{7,6},{8,9},{9,8},{10,11... | collective-permute-start | bytes 6291464 | tf_op jit(solution)/shard_map/ppermute | solution.py:55
  240.7 23.0 %collective-permute-start.47 = (bf16[256,128]{1,0:T(8,128)(2,1)S(1)}, bf16[256,128]{1,0:T(8,128)(2,1)S(1)}, u32[]{:S(2)}, u32[]{:S(2)}) collective-permute-start(bf16[256,128]{1,0:T(8,128)(2,1)S(1)} %get-tuple-element.109), channel_id=1, source_target_pairs={{0,96},{32,0},{64,32},{96,64},{1,97},{33,1},{65,33},{97,65},{2,98}... | collective-permute-start | bytes 196616 | tf_op jit(solution)/shard_map/ppermute | solution.py:70
  263.7 47.2 %collective-permute-start.41 = (bf16[512,2048]{1,0:T(8,128)(2,1)}, bf16[512,2048]{1,0:T(8,128)(2,1)}, u32[]{:S(2)}, u32[]{:S(2)}) collective-permute-start(bf16[512,2048]{1,0:T(8,128)(2,1)} %pad_maximum_fusion.2), channel_id=1, source_target_pairs={{0,1},{1,0},{2,3},{3,2},{4,5},{5,4},{6,7},{7,6},{8,9},{9,8},{10,11... | collective-permute-start | bytes 6291464 | tf_op jit(solution)/shard_map/ppermute | solution.py:55
  264.7 57.4 %collective-permute-start.30 = (bf16[128,2048]{1,0:T(8,128)(2,1)}, bf16[128,2048]{1,0:T(8,128)(2,1)}, u32[]{:S(2)}, u32[]{:S(2)}) collective-permute-start(bf16[128,2048]{1,0:T(8,128)(2,1)} %get-tuple-element.41), channel_id=1, source_target_pairs={{0,96},{32,0},{64,32},{96,64},{1,97},{33,1},{65,33},{97,65},{2,98}... | collective-permute-start | bytes 1572872 | tf_op jit(solution)/shard_map/ppermute | solution.py:70
  273.0 49.1 %collective-permute-start.29 = (bf16[128,2048]{1,0:T(8,128)(2,1)}, bf16[128,2048]{1,0:T(8,128)(2,1)}, u32[]{:S(2)}, u32[]{:S(2)}) collective-permute-start(bf16[128,2048]{1,0:T(8,128)(2,1)} %get-tuple-element.41), channel_id=1, source_target_pairs={{0,64},{32,96},{64,0},{96,32},{1,65},{33,97},{65,1},{97,33},{2,66}... | collective-permute-start | bytes 1572872 | tf_op jit(solution)/shard_map/ppermute | solution.py:70
  276.3 45.8 %collective-permute-start.28 = (bf16[128,2048]{1,0:T(8,128)(2,1)}, bf16[128,2048]{1,0:T(8,128)(2,1)}, u32[]{:S(2)}, u32[]{:S(2)}) collective-permute-start(bf16[128,2048]{1,0:T(8,128)(2,1)} %get-tuple-element.41), channel_id=1, source_target_pairs={{0,32},{32,64},{64,96},{96,0},{1,33},{33,65},{65,97},{97,1},{2,34}... | collective-permute-start | bytes 1572872 | tf_op jit(solution)/shard_map/ppermute | solution.py:70
  296.3 246.1 %reduce-scatter.6.cloned.1.call-start = ((), (), s32[]{:S(2)}) async-start(), calls=%async_computation.10 | async-start | bytes 2359296 | tf_op jit(solution)/shard_map/reduce_scatter | solution.py:110
  319.5 23.4 %collective-permute-start.23 = (bf16[128,2048]{1,0:T(8,128)(2,1)S(1)}, bf16[128,2048]{1,0:T(8,128)(2,1)S(1)}, u32[]{:S(2)}, u32[]{:S(2)}) collective-permute-start(bf16[128,2048]{1,0:T(8,128)(2,1)S(1)} %copy-done.16), channel_id=1, source_target_pairs={{0,96},{32,0},{64,32},{96,64},{1,97},{33,1},{65,33},{97,65},{2,98}... | collective-permute-start | bytes 1572872 | tf_op jit(solution)/shard_map/ppermute | solution.py:70
  321.2 21.7 %collective-permute-start.22 = (bf16[128,2048]{1,0:T(8,128)(2,1)S(1)}, bf16[128,2048]{1,0:T(8,128)(2,1)S(1)}, u32[]{:S(2)}, u32[]{:S(2)}) collective-permute-start(bf16[128,2048]{1,0:T(8,128)(2,1)S(1)} %copy-done.16), channel_id=1, source_target_pairs={{0,64},{32,96},{64,0},{96,32},{1,65},{33,97},{65,1},{97,33},{2,66}... | collective-permute-start | bytes 1572872 | tf_op jit(solution)/shard_map/ppermute | solution.py:70
  322.1 23.8 %collective-permute-start.21 = (bf16[128,2048]{1,0:T(8,128)(2,1)S(1)}, bf16[128,2048]{1,0:T(8,128)(2,1)S(1)}, u32[]{:S(2)}, u32[]{:S(2)}) collective-permute-start(bf16[128,2048]{1,0:T(8,128)(2,1)S(1)} %copy-done.16), channel_id=1, source_target_pairs={{0,32},{32,64},{64,96},{96,0},{1,33},{33,65},{65,97},{97,1},{2,34}... | collective-permute-start | bytes 1572872 | tf_op jit(solution)/shard_map/ppermute | solution.py:70
  325.2 83.6 %collective-permute-start.34 = (bf16[512,2048]{1,0:T(8,128)(2,1)}, bf16[512,2048]{1,0:T(8,128)(2,1)}, u32[]{:S(2)}, u32[]{:S(2)}) collective-permute-start(bf16[512,2048]{1,0:T(8,128)(2,1)} %pad_maximum_fusion.1), channel_id=1, source_target_pairs={{0,1},{1,0},{2,3},{3,2},{4,5},{5,4},{6,7},{7,6},{8,9},{9,8},{10,11... | collective-permute-start | bytes 6291464 | tf_op jit(solution)/shard_map/ppermute | solution.py:55
  325.6 30.3 %collective-permute-start.33 = (bf16[256,1024]{1,0:T(8,128)(2,1)S(1)}, bf16[256,1024]{1,0:T(8,128)(2,1)S(1)}, u32[]{:S(2)}, u32[]{:S(2)}) collective-permute-start(bf16[256,1024]{1,0:T(8,128)(2,1)S(1)} %pad_maximum_fusion.11), channel_id=1, source_target_pairs={{0,96},{32,0},{64,32},{96,64},{1,97},{33,1},{65,33},{97,65},{2,98}... | collective-permute-start | bytes 1572872 | tf_op jit(solution)/shard_map/ppermute | solution.py:70
  347.4 133.2 %collective-permute-start.27 = (bf16[512,2048]{1,0:T(8,128)(2,1)}, bf16[512,2048]{1,0:T(8,128)(2,1)}, u32[]{:S(2)}, u32[]{:S(2)}) collective-permute-start(bf16[512,2048]{1,0:T(8,128)(2,1)} %pad_maximum_fusion), channel_id=1, source_target_pairs={{0,1},{1,0},{2,3},{3,2},{4,5},{5,4},{6,7},{7,6},{8,9},{9,8},{10,11... | collective-permute-start | bytes 6291464 | tf_op jit(solution)/shard_map/ppermute | solution.py:55
  404.1 35.7 %all-to-all-start.3 = ((bf16[16,2,256,128]{3,2,1,0:T(8,128)(2,1)}), bf16[16,2,256,128]{3,2,1,0:T(8,128)(2,1)}, u32[]{:S(2)}, u32[]{:S(2)}) async-start(bf16[16,2,256,128]{3,2,1,0:T(8,128)(2,1)} %bitcast.168), calls=%async_computation.3 | async-start | bytes 4194304 | tf_op jit(solution)/shard_map/all_to_all | solution.py:51
  408.8 145.2 %reduce-scatter.4.cloned.1.call-start = ((), (), s32[]{:S(2)}) async-start(), calls=%async_computation.9 | async-start | bytes 4718592 | tf_op jit(solution)/shard_map/reduce_scatter | solution.py:110
  420.1 115.8 %collective-permute-start.9 = (bf16[128,2048]{1,0:T(8,128)(2,1)}, bf16[128,2048]{1,0:T(8,128)(2,1)}, u32[]{:S(2)}, u32[]{:S(2)}) collective-permute-start(bf16[128,2048]{1,0:T(8,128)(2,1)} %get-tuple-element.62), channel_id=1, source_target_pairs={{0,1},{1,0},{2,3},{3,2},{4,5},{5,4},{6,7},{7,6},{8,9},{9,8},{10,11... | collective-permute-start | bytes 1572872 | tf_op jit(solution)/shard_map/ppermute | solution.py:55
  460.0 31.3 %collective-permute-start.18 = (bf16[128,2048]{1,0:T(8,128)(2,1)S(1)}, bf16[128,2048]{1,0:T(8,128)(2,1)S(1)}, u32[]{:S(2)}, u32[]{:S(2)}) collective-permute-start(bf16[128,2048]{1,0:T(8,128)(2,1)S(1)} %slice.647), channel_id=1, source_target_pairs={{0,1},{1,0},{2,3},{3,2},{4,5},{5,4},{6,7},{7,6},{8,9},{9,8},{10,11... | collective-permute-start | bytes 1572872 | tf_op jit(solution)/shard_map/ppermute | solution.py:55
  486.3 54.3 %all-to-all-start.4 = ((bf16[32,64,384]{2,1,0:T(8,128)(2,1)}), bf16[32,64,384]{2,1,0:T(8,128)(2,1)}, u32[]{:S(2)}, u32[]{:S(2)}) async-start(bf16[32,64,384]{2,1,0:T(8,128)(2,1)} %bitcast.177), calls=%async_computation.4 | async-start | bytes 3145728 | tf_op jit(solution)/shard_map/all_to_all | solution.py:51
  492.8 46.7 %collective-permute-start.19 = (bf16[128,2048]{1,0:T(8,128)(2,1)S(1)}, bf16[128,2048]{1,0:T(8,128)(2,1)S(1)}, u32[]{:S(2)}, u32[]{:S(2)}) collective-permute-start(bf16[128,2048]{1,0:T(8,128)(2,1)S(1)} %fusion.15), channel_id=1, source_target_pairs={{0,2},{2,0},{1,3},{3,1},{4,6},{6,4},{5,7},{7,5},{8,10},{10,8},{9,1... | collective-permute-start | bytes 1572872 | tf_op jit(solution)/shard_map/ppermute | solution.py:55
  493.6 36.2 %collective-permute-start.52 = (f32[5120]{0:T(1024)S(1)}, f32[5120]{0:T(1024)S(1)}, u32[]{:S(2)}, u32[]{:S(2)}) collective-permute-start(f32[5120]{0:T(1024)S(1)} %add.277), channel_id=1, source_target_pairs={{0,16},{16,0},{1,17},{17,1},{2,18},{18,2},{3,19},{19,3},{4,20},{20... | collective-permute-start | bytes 61448 | tf_op jit(solution)/shard_map/ppermute | solution.py:120
  540.0 22.4 %collective-permute-start.20 = (f32[128,2048]{1,0:T(8,128)S(1)}, f32[128,2048]{1,0:T(8,128)}, u32[]{:S(2)}, u32[]{:S(2)}) collective-permute-start(f32[128,2048]{1,0:T(8,128)S(1)} %add_add_fusion), channel_id=1, source_target_pairs={{0,1},{1,0},{2,3},{3,2},{4,5},{5,4},{6,7},{7,6},{8,9},{9,8},{10,11... | collective-permute-start | bytes 3145736 | tf_op jit(solution)/shard_map/ppermute | solution.py:55
  (99 other events, 1127.0 us)
Sparse Core Ops, SparseCore 0:
  296.4 70.2 reduce-scatter.7
  370.9 77.5 reduce-scatter.5
  452.8 101.1 reduce-scatter.3
